TPU v7x, 32 devices: a whole 2x2x4 slice. The times are simulated.
32 devices in a mesh: space: 8 (over z, y), member: 4 (over x, core).
Axes of the slice: x: 2, y: 2, z: 4, core: 2. Of those that a mesh axis runs over, the one named last changes fastest.
Arguments:
- start_temp: float32 [4, 16, 512, 128], P('member', None, 'space'), may hold values from -6 to 6
- cotangent: float32 [4, 16, 512, 128], P('member', None, 'space'), may hold values from -6 to 6
- conductivity: float32 [16, 512, 128], P(None, 'space'), may hold values from 1 to 4
- porosity: float32 [16, 512, 128], P(None, 'space'), may hold values from 0.02 to 0.3
- surface_temp: float32 [4, 512, 128], P('member', 'space'), may hold values from -8 to 8
- surface_offset: float32 [512, 128], P('space'), may hold values from -6 to 6
- basal_flux: float32 [512, 128], P('space'), may hold values from 1 to 6
- thickness: float32 [512, 128], P('space'), may hold values from 0.7 to 1.4
- tile_len: int32 [8], P('space'), may hold values from 1 to 64, 384 in all
Outputs:
- heated: float32 [4, 16, 512, 128], P('member', None, 'space')
- adj_temp: float32 [4, 16, 512, 128], P('member', None, 'space')
- new_cond: float32 [16, 512, 128], P(None, 'space')
- grad_offset: float32 [512, 128], P('space')
Inputs may be any that keep to these rules, and one draw needn't show every extreme that they name: `tile_len`: the largest tile has exactly 64 live rows, and all tiles together hold 384 live rows.
All inputs are finite; a program needn't handle non-finite values. No bound on the sum of `tile_len` on one device may be relied on, other than what follows from the above.
Results may differ from a plain program's by a relative error of at most 0.00002.
Values sent between devices are 32-bit elements; how exact they have to be, the bound alone decides.
A program may use at most 64 MiB of HBM per device.

v0:
```python
import jax
import jax.numpy as jnp
from jax import lax
from jax.sharding import PartitionSpec as P

WIDTH_T = 0.5
LATENT = 16.0
STEP = 0.03
RATE = 0.5


def from_behind(block, axis, distance):
    devices = range(lax.axis_size(axis))
    route = [(i - distance, i) for i in devices if i - distance in devices]
    return lax.ppermute(block, axis, route)


def tendency(temp, cond, prev_t, prev_k, next_t, next_k, porosity, surf, basal, thickness, live):
    flow = 0.5 * (cond + prev_k) * (prev_t - temp) + 0.5 * (cond + next_k) * (next_t - temp)
    west_t = jnp.concatenate([temp[..., :1], temp[..., :-1]], axis=-1)
    west_k = jnp.concatenate([cond[..., :1], cond[..., :-1]], axis=-1)
    east_t = jnp.concatenate([temp[..., 1:], temp[..., -1:]], axis=-1)
    east_k = jnp.concatenate([cond[..., 1:], cond[..., -1:]], axis=-1)
    flow = flow + 0.5 * (cond + west_k) * (west_t - temp) + 0.5 * (cond + east_k) * (east_t - temp)
    inverse = 1.0 / (thickness * thickness)
    upper_t = jnp.concatenate([temp[:1], temp[:-1]], axis=0)
    upper_k = jnp.concatenate([cond[:1], cond[:-1]], axis=0)
    lower_t = jnp.concatenate([temp[1:], temp[-1:]], axis=0)
    lower_k = jnp.concatenate([cond[1:], cond[-1:]], axis=0)
    vertical = 0.5 * (cond + upper_k) * (upper_t - temp) + 0.5 * (cond + lower_k) * (lower_t - temp)
    flow = flow + vertical * inverse[None]
    layer = jnp.arange(temp.shape[0], dtype=jnp.int32)[:, None, None]
    flow = flow + jnp.where(layer == 0, 2.0 * cond * inverse[None] * (surf[None] - temp), 0.0)
    flow = flow + jnp.where(layer == temp.shape[0] - 1, (basal / thickness)[None], 0.0)
    sig = jax.nn.sigmoid(temp / WIDTH_T)
    capacity = 1.0 + LATENT * porosity * sig * (1.0 - sig)
    return jnp.where(live, temp + STEP * flow / capacity, 0.0)


def body(
    start_temp,
    cotangent,
    conductivity,
    porosity,
    surface_temp,
    surface_offset,
    basal_flux,
    thickness,
    tile_len,
):
    temp = start_temp[0]
    cot = cotangent[0]
    surf_base = surface_temp[0]
    layers, rows, across = temp.shape
    count = tile_len[0]
    row_ids = jnp.arange(rows, dtype=jnp.int32)
    at_end = (row_ids == count - 1)[None, :, None]
    live = (row_ids < count)[None, :, None]
    stacked = jnp.stack([temp, conductivity])
    last_row = lax.dynamic_slice_in_dim(stacked, count - 1, 1, 2)[:, :, 0]
    first_row = stacked[:, :, 0]
    from_left = from_behind(last_row, "space", 1)
    from_right = from_behind(first_row, "space", -1)
    blank = jnp.zeros((layers, 1, across), jnp.float32)

    def local(field, cond, halo_prev, halo_next, offset):
        prev_t = jnp.concatenate([halo_prev[0][:, None], field[:, :-1]], axis=1)
        prev_k = jnp.concatenate([halo_prev[1][:, None], cond[:, :-1]], axis=1)
        next_t = jnp.where(
            at_end, halo_next[0][:, None], jnp.concatenate([field[:, 1:], blank], axis=1)
        )
        next_k = jnp.where(
            at_end, halo_next[1][:, None], jnp.concatenate([cond[:, 1:], blank], axis=1)
        )
        return tendency(
            field,
            cond,
            prev_t,
            prev_k,
            next_t,
            next_k,
            porosity,
            surf_base + offset,
            basal_flux,
            thickness,
            live,
        )

    heated, pull = jax.vjp(local, temp, conductivity, from_left, from_right, surface_offset)
    grad_t, grad_k, grad_prev, grad_next, grad_off = pull(cot)
    back_last = from_behind(grad_prev, "space", -1)
    back_first = from_behind(grad_next, "space", 1)
    grad_t = grad_t + jnp.where(at_end, back_last[0][:, None], 0.0)
    grad_t = grad_t.at[:, 0].add(back_first[0])
    grad_k = grad_k + jnp.where(at_end, back_last[1][:, None], 0.0)
    grad_k = grad_k.at[:, 0].add(back_first[1])
    total_k, total_off = lax.psum((grad_k, grad_off), "member")
    new_cond = conductivity * jnp.exp(-RATE * jnp.tanh(total_k))
    return (heated[None], grad_t[None], new_cond, total_off)


def solution(mesh):
    in_specs = (
        P("member", None, "space", None),
        P("member", None, "space", None),
        P(None, "space", None),
        P(None, "space", None),
        P("member", "space", None),
        P("space", None),
        P("space", None),
        P("space", None),
        P("space"),
    )
    out_specs = (
        P("member", None, "space", None),
        P("member", None, "space", None),
        P(None, "space", None),
        P("space", None),
    )
    return jax.shard_map(body, mesh=mesh, in_specs=in_specs, out_specs=out_specs, check_vma=False)
```

profile of v0, /device:TPU:0, one launch (start us, length us, event | category | flops | bytes accessed | tf_op | source)
XLA Modules:
  0.0 110.9 jit_solution(685442951797498015)
XLA Ops:
  7.9 1.0 pad_maximum_fusion
  8.9 4.9 %collective-permute-start = (f32[2,16,128]{2,1,0:T(8,128)S(1)}, f32[2,16,128]{2,1,0:T(8,128)S(1)}, u32[]{:S(2)}, u32[]{:S(2)}) collective-permute-start(f32[2,16,128]{2,1,0:T(8,128)S(1)} %bitcast.119), channel_id=1, source_target_pairs={{0,4},{4,8},{8,12},{12,16},{16,20},{20,24},{24,28},{1,5},{5,9},{9,... | collective-permute-start | bytes 49160 | tf_op jit(solution)/shard_map/ppermute | solution.py:15
  13.8 1.3 %collective-permute-start.1 = (f32[2,16,128]{2,1,0:T(8,128)S(1)}, f32[2,16,128]{2,1,0:T(8,128)S(1)}, u32[]{:S(2)}, u32[]{:S(2)}) collective-permute-start(f32[2,16,128]{2,1,0:T(8,128)S(1)} %bitcast.118), channel_id=1, source_target_pairs={{4,0},{8,4},{12,8},{16,12},{20,16},{24,20},{28,24},{5,1},{9,5},{13... | collective-permute-start | bytes 49160 | tf_op jit(solution)/shard_map/ppermute | solution.py:15
  15.4 0.7 copy-done
  16.2 1.0 fusion.52
  17.2 1.1 %fusion.48 = (f32[15,64,128]{2,1,0:T(8,128)}, f32[15,64,128]{2,1,0:T(8,128)}) fusion(f32[16,64,128]{2,1,0:T(8,128)S(1)} %copy-done), kind=kLoop, calls=%fused_computation.110 | loop fusion | bytes 1966080 | tf_op jit(solution)/shard_map/jvp()/slice | solution.py:29
  18.3 1.1 %fusion.51 = (f32[16,64,1]{2,1,0:T(8,128)}, f32[16,64,1]{2,1,0:T(8,128)}) fusion(f32[16,64,128]{2,1,0:T(8,128)S(1)} %copy-done), kind=kLoop, calls=%fused_computation.113 | loop fusion | bytes 16384 | tf_op jit(solution)/shard_map/jvp()/slice | solution.py:23
  19.5 1.1 %fusion.50 = (f32[16,64,127]{2,1,0:T(8,128)}, f32[16,64,127]{2,1,0:T(8,128)}) fusion(f32[16,64,128]{2,1,0:T(8,128)S(1)} %copy-done), kind=kLoop, calls=%fused_computation.112 | loop fusion | bytes 2080768 | tf_op jit(solution)/shard_map/jvp()/slice | solution.py:23
  20.6 1.1 slice_bitcast_fusion.1
  21.7 1.1 fusion.47
  23.0 1.0 fusion.44
  24.0 0.7 copy-done.21
  24.8 1.5 %fusion.36 = (f32[64,128]{1,0:T(8,128)S(1)}, f32[16,64,128]{2,0,1:T(8,128)S(1)}) fusion(pred[16]{0:T(512)(128)(4,1)S(1)} %iota_compare_fusion.1, f32[64,128]{1,0:T(8,128)S(1)} %get-tuple-element.86, f32[16,64,128]{2,1,0:T(8,128)S(1)} %copy-done, f32[1,16,64,128]{3,2,1,0:T(8,128)S(1)} %copy-done.1, f32[16,64,128]{2,1,0:T(8,128)S(1)} %copy-done.6, ...), kind=kLoop, calls=%fused_computation.80 | loop fusion | flops 2088960 | bytes 2687056 | tf_op jit(solution)/shard_map/transpose(jvp())/reduce_sum | solution.py:33
  26.3 11.4 %psum.15 = f32[64,128]{1,0:T(8,128)} all-reduce(f32[64,128]{1,0:T(8,128)S(1)} %get-tuple-element.38), channel_id=1, replica_groups=mesh['space'=8,'member'=4] {'member'}, use_global_device_ids=true, to_apply=%region_4.5 | all-reduce | flops 8192 | bytes 65536 | tf_op jit(solution)/shard_map/psum | solution.py:97
  37.7 1.4 %copy.148 = f32[16,63,128]{2,0,1:T(8,128)S(1)} copy(f32[16,63,128]{2,1,0:T(8,128)} %get-tuple-element.83) | data formatting | bytes 1032192
  39.4 0.7 copy-done.19
  40.8 0.7 copy-done.17
  41.8 0.7 copy-done.16
  42.9 0.7 copy-done.14
  43.9 0.7 copy-done.13
  46.9 1.3 %multiply_multiply_fusion.3 = (f32[16,64,128]{2,0,1:T(8,128)S(1)}, f32[16,64,128]{2,0,1:T(8,128)S(1)}, f32[16,64,128]{2,0,1:T(8,128)S(1)}, f32[16,128]{1,0:T(8,1...) fusion(f32[16,64,128]{2,0,1:T(8,128)S(1)} %get-tuple-element.39, ...), kind=kLoop, calls=%fused_computation.56 | loop fusion | flops 4452352 | bytes 8962112 | tf_op jit(solution)/shard_map/transpose(jvp())/mul | solution.py:30
  48.3 1.3 %collective-permute-start.2 = (f32[2,16,128]{2,1,0:T(8,128)S(1)}, f32[2,16,128]{2,1,0:T(8,128)S(1)}, u32[]{:S(2)}, u32[]{:S(2)}) collective-permute-start(f32[2,16,128]{2,1,0:T(8,128)S(1)} %pad_add_fusion.2), channel_id=1, source_target_pairs={{4,0},{8,4},{12,8},{16,12},{20,16},{24,20},{28,24},{5,1},{9,5},{13... | collective-permute-start | bytes 49160 | tf_op jit(solution)/shard_map/ppermute | solution.py:15
  50.2 5.1 %collective-permute-start.3 = (f32[2,16,128]{2,1,0:T(8,128)S(1)}, f32[2,16,128]{2,1,0:T(8,128)S(1)}, u32[]{:S(2)}, u32[]{:S(2)}) collective-permute-start(f32[2,16,128]{2,1,0:T(8,128)S(1)} %pad_add_fusion.1), channel_id=1, source_target_pairs={{0,4},{4,8},{8,12},{12,16},{16,20},{20,24},{24,28},{1,5},{5,9},{9,... | collective-permute-start | bytes 49160 | tf_op jit(solution)/shard_map/ppermute | solution.py:15
  55.5 0.8 copy-done.2
  56.7 5.9 %fusion.23 = (f32[16,64,128]{2,0,1:T(8,128)}, f32[16,64,128]{2,0,1:T(8,128)S(1)}) fusion(f32[16,63,128]{2,0,1:T(8,128)S(1)} %split.83, f32[16,63,128]{2,0,1:T(8,128)S(1)} %get-tuple-element.96, f32[16,64,128]{2,0,1:T(8,128)S(1)} %get-tuple-element.50, f32[16,64,128]{2,0,1:T(8,128)S(1)} %get-tuple-element.58, f32[16,64,127]{2,0,1:T(8,128)S(1)} %split.81, ...), kind=kLoop, calls=%fused_computation.28 | loop fusion | flops 13893632 | bytes 15814960 | tf_op jit(solution)/shard_map/add | solution.py:93
  62.5 1.8 %multiply_multiply_fusion.1 = (f32[16,64,128]{2,0,1:T(8,128)S(1)}, f32[16,64,128]{2,0,1:T(8,128)S(1)}, f32[16,64,128]{2,0,1:T(8,128)}) fusion(f32[16,64,128]{2,0,1:T(8,128)S(1)} %get-tuple-element.39, f32[16,64,1]{2,0,1:T(8,128)S(1)} %get-tuple-element.64, f32[16,64,127]{2,0,1:T(8,128)S(1)} %copy-done.2, f32[1,16,64,128]{3,2,1,0:T(8,128)S(1)} %copy-done.1, ...), kind=kLoop, calls=%fused_computation.54 | loop fusion | flops 2621440 | bytes 4718592 | tf_op jit(solution)/shard_map/transpose(jvp())/mul | solution.py:24
  64.7 1.3 %pad_add_fusion = f32[16,64,128]{2,0,1:T(8,128)S(1)} fusion(f32[16,63,128]{2,0,1:T(8,128)S(1)} %split.93, f32[16,63,128]{2,0,1:T(8,128)S(1)} %get-tuple-element.95, f32[16,64,128]{2,0,1:T(8,128)S(1)} %get-tuple-element.52, f32[16,64,127]{2,0,1:T(8,128)S(1)} %split.91, f32[16,64,127]{2,0,1:T(8,128)S(1)} %bitcast.105, f32[16,64,1]{2,0,1:T(8,128)S(1)} %split.89, ...), kind=kLoop, calls=%fused_computation.52 | loop fusion | flops 4718592 | bytes 7876768 | tf_op jit(solution)/shard_map/transpose(jvp())/add_any | solution.py:68
  66.3 0.8 copy-done.10
  67.4 1.0 copy.77
  68.4 1.0 fusion.29
  69.4 32.6 %all-reduce.24.cloned.1.call-done = f32[16,64,128]{2,1,0:T(8,128)} async-done(((f32[16,64,128]{2,1,0:T(8,128)}), f32[16,64,128]{2,1,0:T(8,128)}) %all-reduce.24.cloned.1.call-update) | async-done | bytes 524304 | tf_op jit(solution)/shard_map/psum | solution.py:97
  102.1 2.0 %exponential_multiply_fusion = f32[16,64,128]{2,1,0:T(8,128)} fusion(f32[16,64,128]{2,1,0:T(8,128)S(1)} %copy-done, f32[16,64,128]{2,1,0:T(8,128)} %all-reduce.24.cloned.1.call-done), kind=kLoop, calls=%fused_computation.51 | loop fusion | flops 262144 | bytes 1572864 | tf_op jit(solution)/shard_map/mul | solution.py:98
  (93 shorter events, 6.8 us)
Async XLA Ops:
  7.2 94.9 %all-reduce.24.cloned.1.call-start = ((), (), s32[]{:S(2)}) async-start(), calls=%async_computation | async-start | bytes 1048576 | tf_op jit(solution)/shard_map/psum | solution.py:97
  7.9 7.2 %copy-start.1 = (f32[1,16,64,128]{3,2,1,0:T(8,128)S(1)}, f32[1,16,64,128]{3,2,1,0:T(8,128)}, u32[]{:S(2)}) copy-start(f32[1,16,64,128]{3,2,1,0:T(8,128)} %param.13) | copy-start | bytes 1572868
  8.9 36.0 %collective-permute-start = (f32[2,16,128]{2,1,0:T(8,128)S(1)}, f32[2,16,128]{2,1,0:T(8,128)S(1)}, u32[]{:S(2)}, u32[]{:S(2)}) collective-permute-start(f32[2,16,128]{2,1,0:T(8,128)S(1)} %bitcast.119), channel_id=1, source_target_pairs={{0,4},{4,8},{8,12},{12,16},{16,20},{20,24},{24,28},{1,5},{5,9},{9,... | collective-permute-start | bytes 49160 | tf_op jit(solution)/shard_map/ppermute | solution.py:15
  13.8 31.9 %collective-permute-start.1 = (f32[2,16,128]{2,1,0:T(8,128)S(1)}, f32[2,16,128]{2,1,0:T(8,128)S(1)}, u32[]{:S(2)}, u32[]{:S(2)}) collective-permute-start(f32[2,16,128]{2,1,0:T(8,128)S(1)} %bitcast.118), channel_id=1, source_target_pairs={{4,0},{8,4},{12,8},{16,12},{20,16},{24,20},{28,24},{5,1},{9,5},{13... | collective-permute-start | bytes 49160 | tf_op jit(solution)/shard_map/ppermute | solution.py:15
  15.1 1.0 copy-start
  22.9 1.1 copy-start.23
  22.9 1.1 copy-start.24
  22.9 1.8 %copy-start.6 = (f32[16,64,128]{2,1,0:T(8,128)S(1)}, f32[16,64,128]{2,1,0:T(8,128)}, u32[]{:S(2)}) copy-start(f32[16,64,128]{2,1,0:T(8,128)} %param.16) | copy-start | bytes 1572868
  22.9 1.8 %copy-start.11 = (f32[1,16,64,128]{3,2,1,0:T(8,128)S(1)}, f32[1,16,64,128]{3,2,1,0:T(8,128)}, u32[]{:S(2)}) copy-start(f32[1,16,64,128]{3,2,1,0:T(8,128)} %param.14) | copy-start | bytes 1572868
  24.0 0.8 copy-start.21
  24.0 0.8 copy-start.22
  37.7 1.4 %copy-start.20 = (f32[15,64,128]{2,1,0:T(8,128)S(1)}, f32[15,64,128]{2,1,0:T(8,128)}, u32[]{:S(2)}) copy-start(f32[15,64,128]{2,1,0:T(8,128)} %get-tuple-element.75) | copy-start | bytes 1474564
  39.1 1.0 copy-start.19
  39.4 1.1 copy-start.15
  40.5 1.0 copy-start.17
  41.5 1.0 copy-start.16
  42.5 1.0 copy-start.14
  43.6 1.0 copy-start.13
  45.0 1.0 copy-start.5
  45.0 1.2 %copy-start.8 = (f32[16,63,128]{2,0,1:T(8,128)S(1)}, f32[16,63,128]{2,0,1:T(8,128)}, u32[]{:S(2)}) copy-start(f32[16,63,128]{2,0,1:T(8,128)} %get-tuple-element.74) | copy-start | bytes 1548292
  45.6 1.1 %copy-start.3 = (f32[16,63,128]{2,0,1:T(8,128)S(1)}, f32[16,63,128]{2,0,1:T(8,128)}, u32[]{:S(2)}) copy-start(f32[16,63,128]{2,0,1:T(8,128)} %get-tuple-element.73) | copy-start | bytes 1548292
  45.6 1.3 %copy-start.4 = (f32[15,64,128]{2,0,1:T(8,128)S(1)}, f32[15,64,128]{2,0,1:T(8,128)}, u32[]{:S(2)}) copy-start(f32[15,64,128]{2,0,1:T(8,128)} %get-tuple-element.69) | copy-start | bytes 1474564
  48.3 7.2 %collective-permute-start.2 = (f32[2,16,128]{2,1,0:T(8,128)S(1)}, f32[2,16,128]{2,1,0:T(8,128)S(1)}, u32[]{:S(2)}, u32[]{:S(2)}) collective-permute-start(f32[2,16,128]{2,1,0:T(8,128)S(1)} %pad_add_fusion.2), channel_id=1, source_target_pairs={{4,0},{8,4},{12,8},{16,12},{20,16},{24,20},{28,24},{5,1},{9,5},{13... | collective-permute-start | bytes 49160 | tf_op jit(solution)/shard_map/ppermute | solution.py:15
  50.2 16.0 %collective-permute-start.3 = (f32[2,16,128]{2,1,0:T(8,128)S(1)}, f32[2,16,128]{2,1,0:T(8,128)S(1)}, u32[]{:S(2)}, u32[]{:S(2)}) collective-permute-start(f32[2,16,128]{2,1,0:T(8,128)S(1)} %pad_add_fusion.1), channel_id=1, source_target_pairs={{0,4},{4,8},{8,12},{12,16},{16,20},{20,24},{24,28},{1,5},{5,9},{9,... | collective-permute-start | bytes 49160 | tf_op jit(solution)/shard_map/ppermute | solution.py:15
  55.3 1.0 copy-start.2
  55.3 1.2 %copy-start.7 = (f32[16,64,128]{2,1,0:T(8,128)S(1)}, f32[16,64,128]{2,1,0:T(8,128)}, u32[]{:S(2)}) copy-start(f32[16,64,128]{2,1,0:T(8,128)} %param.16) | copy-start | bytes 1572868
  55.3 1.3 %copy-start.12 = (f32[1,16,64,128]{3,2,1,0:T(8,128)S(1)}, f32[1,16,64,128]{3,2,1,0:T(8,128)}, u32[]{:S(2)}) copy-start(f32[1,16,64,128]{3,2,1,0:T(8,128)} %param.14) | copy-start | bytes 1572868
  55.5 1.2 %copy-start.25 = (pred[16]{0:T(512)(128)(4,1)S(1)}, pred[16]{0:T(512)(128)(4,1)}, u32[]{:S(2)}) copy-start(pred[16]{0:T(512)(128)(4,1)} %constant.89.clone.1) | copy-start | bytes 52
  55.5 1.1 %copy-start.26 = (pred[128]{0:T(512)(128)(4,1)S(1)}, pred[128]{0:T(512)(128)(4,1)}, u32[]{:S(2)}) copy-start(pred[128]{0:T(512)(128)(4,1)} %constant.90.clone.1) | copy-start | bytes 388
  66.2 1.1 %copy-start.9 = (f32[16,64,128]{2,0,1:T(8,128)S(1)}, f32[16,64,128]{2,0,1:T(8,128)}, u32[]{:S(2)}) copy-start(f32[16,64,128]{2,0,1:T(8,128)} %get-tuple-element.42) | copy-start | bytes 1572868
  66.3 0.8 copy-start.10
  67.4 1.0 copy-start.18
Sparse Core Ops, SparseCore 0:
  67.3 34.7 all-reduce.23
where the time goes:
time: 112 us; the launch traced here: 111 us
  waiting for transfers between devices  32.7 us (29%)
  local copies, waits for them, and re-layouts  22.3 us (20%)
  other arithmetic  16.8 us (15%)
  between operations  15.2 us (14%)
  starting transfers between devices  12.6 us (11%)
  blocking collectives  11.4 us (10%)
    psum x1, waiting for transfers between devices, body(): total_k, total_off = lax.psum((grad_k, grad_off), 'member')  32.6 us
    unnamed x65, local copies, waits for them, and re-layouts  13.4 us
    ppermute x4, starting transfers between devices, from_behind(): return lax.ppermute(block, axis, route)  12.5 us
    psum x1, blocking collectives, body(): total_k, total_off = lax.psum((grad_k, grad_off), 'member')  11.4 us
    add x1, other arithmetic, body(): grad_t = grad_t + jnp.where(at_end, back_last[0][:, None], 0.0)  5.86 us
    mul x2, other arithmetic, tendency(): 0.5 * (cond + east_k) * (east_t - temp)  2.41 us
    slice x2, local copies, waits for them, and re-layouts, tendency(): east_k = jnp.concatenate([cond[..., 1:], cond[..., -1:]], axis=-1)  2.25 us
  transfers between devices with their start and end apart: 5, of which 1 were waited for; matrix products, arithmetic and copies ran while one was open for 23% of the time, Pallas kernels for 0%

commit v1 on v0

v1 whole, which is shorter than its diff:
```python
import jax
import jax.numpy as jnp
from jax import lax
from jax.experimental import pallas as pl
from jax.experimental.pallas import tpu as pltpu
from jax.sharding import PartitionSpec as P

STEP = 0.03
RATE = 0.5
MESH = pl.DeviceIdType.MESH
CORES = 2


def kernel(
    n_space,
    groups,
    len_ref,
    temp_hbm,
    por_hbm,
    cot_hbm,
    cond_hbm,
    surf_hbm,
    offset_hbm,
    basal_hbm,
    thick_hbm,
    heated_hbm,
    adj_hbm,
    new_hbm,
    goff_hbm,
    temp,
    por,
    cot,
    cond,
    surf,
    offset,
    basal,
    thick,
    inverse,
    weight,
    recip,
    slope,
    heated,
    adj,
    grad,
    near,
    far,
    new,
    edge_out,
    edge_in,
    edge,
    extra_out,
    extra_near,
    extra_far,
    goff,
    in_sem,
    halo_send,
    halo_recv,
    near_send,
    near_recv,
    far_send,
    far_recv,
    new_send,
    new_recv,
    new_local,
    out_sem,
):
    layers, rows, across = temp.shape
    chunks = layers // CORES
    half = rows // CORES
    space = lax.axis_index("space")
    member = lax.axis_index("member")
    core = lax.rem(member, CORES)
    group = lax.div(member, CORES)
    partner = (space, member + 1 - 2 * core)
    peers = [lax.rem(group + d, groups) for d in range(1, groups)]
    peer_ids = [(space, p * CORES + core) for p in peers]
    behind = (space - 1, member)
    ahead = (space + 1, member)
    has_behind = space > 0
    has_ahead = space < n_space - 1

    barrier = pltpu.get_barrier_semaphore()
    for other in [partner] + peer_ids:
        pl.semaphore_signal(barrier, inc=1, device_id=other, device_id_type=MESH)

    @pl.when(has_behind)
    def _():
        pl.semaphore_signal(barrier, inc=1, device_id=behind, device_id_type=MESH)

    @pl.when(has_ahead)
    def _():
        pl.semaphore_signal(barrier, inc=1, device_id=ahead, device_id_type=MESH)

    loads = [
        pltpu.make_async_copy(src, dst, in_sem.at[i])
        for i, (src, dst) in enumerate(
            [
                (temp_hbm, temp),
                (por_hbm, por),
                (cot_hbm, cot),
                (cond_hbm, cond),
                (surf_hbm, surf),
                (offset_hbm, offset),
                (basal_hbm, basal),
                (thick_hbm, thick),
            ]
        )
    ]
    for load in loads:
        load.start()

    count = len_ref[0]
    end = jnp.clip(count - 1, 0, rows - 1)
    row = lax.broadcasted_iota(jnp.int32, (rows, across), 0)
    col = lax.broadcasted_iota(jnp.int32, (rows, across), 1)
    live = row < count
    inner = (row >= 1) & live
    not_east = col < across - 1

    @pl.when(jnp.logical_not(has_behind))
    def _():
        edge_in[0] = jnp.zeros(edge_in.shape[1:], jnp.float32)

    @pl.when(jnp.logical_not(has_ahead))
    def _():
        edge_in[1] = jnp.zeros(edge_in.shape[1:], jnp.float32)

    for load in loads:
        load.wait()

    def pointwise(v, p, c):
        th = jnp.tanh(v)
        q = p * (1.0 - th * th)
        r = 1.0 / (1.0 + 4.0 * q)
        return r, STEP * c * r, 8.0 * th * q

    for layer in range(layers):
        at = pl.ds(layer, 1)
        for f, field in enumerate((temp, cond, cot, por)):
            edge_out[0, f, at, :] = field[layer, 0:1, :]
            edge_out[1, f, at, :] = field[layer, pl.ds(end, 1), :]
    for side in range(2):
        _, w, _ = pointwise(edge_out[side, 0], edge_out[side, 3], edge_out[side, 2])
        edge_out[side, 2] = w

    neighbours = has_behind.astype(jnp.int32) + has_ahead.astype(jnp.int32)
    pl.semaphore_wait(barrier, groups + neighbours)

    to_behind = pltpu.make_async_remote_copy(
        src_ref=edge_out.at[0, 0:3],
        dst_ref=edge_in.at[1],
        send_sem=halo_send.at[0],
        recv_sem=halo_recv.at[1],
        device_id=behind,
        device_id_type=MESH,
    )
    to_ahead = pltpu.make_async_remote_copy(
        src_ref=edge_out.at[1, 0:3],
        dst_ref=edge_in.at[0],
        send_sem=halo_send.at[1],
        recv_sem=halo_recv.at[0],
        device_id=ahead,
        device_id_type=MESH,
    )

    @pl.when(has_behind)
    def _():
        to_behind.start()

    @pl.when(has_ahead)
    def _():
        to_ahead.start()

    inverse[...] = 1.0 / (thick[...] * thick[...])

    def weigh(layer):
        r, w, s = pointwise(temp[layer], por[layer], cot[layer])
        w = jnp.where(live, w, 0.0)
        recip[layer] = r
        weight[layer] = w
        slope[layer] = w * r * s

    def stencil(layer, above, below, top=False, bottom=False):
        v, k, w = temp[layer], cond[layer], weight[layer]

        def east(x):
            return pltpu.roll(x, across - 1, 1)

        def west(x):
            return pltpu.roll(x, 1, 1)

        def prev(x):
            return pltpu.roll(x, 1, 0)

        def following(x):
            return pltpu.roll(x, rows - 1, 0)

        a = jnp.where(not_east, 0.5 * (k + east(k)), 0.0)
        dv = jnp.where(not_east, east(v) - v, 0.0)
        dw = east(w) - w
        f, b, g = a * dv, a * dw, dv * dw
        flow = f - west(f)
        back = b - west(b)
        cross = g + west(g)

        a = jnp.where(inner, 0.5 * (k + prev(k)), 0.0)
        dv = jnp.where(inner, prev(v) - v, 0.0)
        dw = prev(w) - w
        f, b, g = a * dv, a * dw, dv * dw
        flow = flow + (f - following(f))
        back = back + (b - following(b))
        cross = cross + (g + following(g))

        parts = []
        for other in (above, below):
            if other is not None:
                a = 0.5 * (k + cond[other])
                dv = temp[other] - v
                dw = weight[other] - w
                parts.append((a * dv, a * dw, dv * dw))
        f, b, g = parts[0]
        for more in parts[1:]:
            f, b, g = f + more[0], b + more[1], g + more[2]
        inv = inverse[...]
        if top:
            a = 2.0 * k
            dv = surf[...] + offset[...] - v
            f = f + a * dv
            b = b - a * w
            g = g - 4.0 * (dv * w)
            goff[...] = a * inv * w
        flow = flow + f * inv
        back = back + b * inv
        cross = cross + g * inv
        if bottom:
            flow = flow + basal[...] / thick[...]
        heated[layer] = flow
        adj[layer] = back
        grad[layer] = -0.5 * cross

    def near_copy(j):
        return pltpu.make_async_remote_copy(
            src_ref=grad.at[CORES * j + 1 - core],
            dst_ref=near.at[j],
            send_sem=near_send.at[j],
            recv_sem=near_recv.at[j],
            device_id=partner,
            device_id_type=MESH,
        )

    def far_copies(j):
        return [
            pltpu.make_async_remote_copy(
                src_ref=far.at[group, j],
                dst_ref=far.at[group, j],
                send_sem=far_send.at[d, j],
                recv_sem=far_recv.at[group, j],
                device_id=peer_ids[d],
                device_id_type=MESH,
            )
            for d in range(groups - 1)
        ]

    def far_arrivals(j):
        return [
            pltpu.make_async_remote_copy(
                src_ref=far.at[peers[d], j],
                dst_ref=far.at[peers[d], j],
                send_sem=far_send.at[d, j],
                recv_sem=far_recv.at[peers[d], j],
                device_id=peer_ids[d],
                device_id_type=MESH,
            )
            for d in range(groups - 1)
        ]

    def chunk(j, first=False, last=False):
        layer = CORES * j
        if not last:
            weigh(layer + 2)
            weigh(layer + 3)
        stencil(layer, None if first else layer - 1, layer + 1, top=first)
        stencil(layer + 1, layer, None if last else layer + 2, bottom=last)
        near_copy(j).start()

    def pass_on(j):
        near_copy(j).wait_recv()
        far[group, j] = grad[CORES * j + core] + near[j]
        for copy in far_copies(j):
            copy.start()

    def step(j, carry):
        chunk(j)
        pass_on(j - 1)
        return carry

    extra_near_copy = pltpu.make_async_remote_copy(
        src_ref=extra_out.at[1 - core],
        dst_ref=extra_near,
        send_sem=near_send.at[chunks],
        recv_sem=near_recv.at[chunks],
        device_id=partner,
        device_id_type=MESH,
    )

    def extra_far_copy(d, slot):
        return pltpu.make_async_remote_copy(
            src_ref=extra_far.at[slot],
            dst_ref=extra_far.at[slot],
            send_sem=far_send.at[d, chunks],
            recv_sem=far_recv.at[slot, chunks],
            device_id=peer_ids[d],
            device_id_type=MESH,
        )

    weigh(0)
    weigh(1)
    chunk(0, first=True)
    middle = chunks // 2
    lax.fori_loop(1, middle, step, 0)

    @pl.when(has_ahead)
    def _():
        to_behind.wait_recv()

    @pl.when(has_behind)
    def _():
        to_ahead.wait_recv()

    for side in range(2):
        a = 0.5 * (edge_out[side, 1] + edge_in[side, 1])
        dv = edge_in[side, 0] - edge_out[side, 0]
        dw = edge_in[side, 2] - edge_out[side, 2]
        edge[side, 0] = a * dv
        edge[side, 1] = a * dw
        g = -0.5 * (dv * dw)
        for layer in range(layers):
            at = side * chunks + layer // CORES
            extra_out[layer % CORES, at : at + 1, :] = g[layer : layer + 1, :]
    for h in range(CORES):
        extra_out[h, layers : layers + half, :] = goff[h * half : (h + 1) * half, :]
    extra_near_copy.start()

    lax.fori_loop(middle, chunks - 1, step, 0)
    extra_near_copy.wait_recv()
    extra_far[group] = extra_out[core] + extra_near[...]
    for d in range(groups - 1):
        extra_far_copy(d, group).start()
    chunk(chunks - 1, last=True)
    pass_on(chunks - 2)

    first_row = row == 0
    last_row = row == count - 1

    def out_copies(layer):
        return (
            pltpu.make_async_copy(heated.at[layer], heated_hbm.at[layer], out_sem.at[0, layer]),
            pltpu.make_async_copy(adj.at[layer], adj_hbm.at[layer], out_sem.at[1, layer]),
        )

    def finish(layer, carry):
        at = pl.ds(layer, 1)

        def edges(f):
            return jnp.where(first_row, edge[0, f, at, :], 0.0) + jnp.where(
                last_row, edge[1, f, at, :], 0.0
            )

        flow = heated[layer] + edges(0)
        heated[layer] = jnp.where(live, temp[layer] + STEP * (flow * recip[layer]), 0.0)
        adj[layer] = jnp.where(
            live, cot[layer] + (adj[layer] + edges(1) + slope[layer] * flow), 0.0
        )
        for copy in out_copies(layer):
            copy.start()
        return carry

    lax.fori_loop(0, 4, finish, 0)
    pass_on(chunks - 1)
    lax.fori_loop(4, layers, finish, 0)

    for d in range(groups - 1):
        extra_far_copy(d, peers[d]).wait_recv()
    total = extra_far[0]
    for p in range(1, groups):
        total = total + extra_far[p]
    extra_near[...] = total
    mine = pl.ds(pl.multiple_of(core * half, half), half)
    goff_local = pltpu.make_async_copy(
        extra_near.at[pl.ds(layers, half)], goff_hbm.at[mine], new_local.at[chunks]
    )
    goff_remote = pltpu.make_async_remote_copy(
        src_ref=extra_near.at[pl.ds(layers, half)],
        dst_ref=goff_hbm.at[mine],
        send_sem=new_send.at[chunks],
        recv_sem=new_recv.at[chunks],
        device_id=partner,
        device_id_type=MESH,
    )
    goff_local.start()
    goff_remote.start()

    def new_copies(j):
        layer = CORES * j + core
        return (
            pltpu.make_async_copy(new.at[j], new_hbm.at[layer], new_local.at[j]),
            pltpu.make_async_remote_copy(
                src_ref=new.at[j],
                dst_ref=new_hbm.at[layer],
                send_sem=new_send.at[j],
                recv_sem=new_recv.at[j],
                device_id=partner,
                device_id_type=MESH,
            ),
        )

    def update(j, carry):
        for copy in far_arrivals(j):
            copy.wait_recv()
        total = far[0, j]
        for p in range(1, groups):
            total = total + far[p, j]
        total = total + jnp.where(first_row, extra_near[pl.ds(j, 1), :], 0.0)
        total = total + jnp.where(last_row, extra_near[pl.ds(chunks + j, 1), :], 0.0)
        new[j] = cond[CORES * j + core] * jnp.exp(-RATE * jnp.tanh(total))
        for copy in new_copies(j):
            copy.start()
        return carry

    lax.fori_loop(0, chunks, update, 0)

    def drain(j, carry):
        near_copy(j).wait_send()
        for copy in far_copies(j):
            copy.wait_send()
        local, remote = new_copies(j)
        local.wait()
        remote.wait()
        return carry

    def drain_out(layer, carry):
        for copy in out_copies(layer):
            copy.wait()
        return carry

    @pl.when(has_behind)
    def _():
        to_behind.wait_send()

    @pl.when(has_ahead)
    def _():
        to_ahead.wait_send()

    extra_near_copy.wait_send()
    for d in range(groups - 1):
        extra_far_copy(d, group).wait_send()
    lax.fori_loop(0, layers, drain_out, 0)
    lax.fori_loop(0, chunks, drain, 0)
    goff_local.wait()
    goff_remote.wait()


def solution(mesh):
    n_space, n_member = mesh.shape["space"], mesh.shape["member"]
    groups = n_member // CORES

    def body(
        start_temp,
        cotangent,
        conductivity,
        porosity,
        surface_temp,
        surface_offset,
        basal_flux,
        thickness,
        tile_len,
    ):
        layers, rows, across = conductivity.shape
        chunks = layers // CORES
        half = rows // CORES
        extra = layers + half
        f32 = jnp.float32
        whole = (layers, rows, across)
        plane = (rows, across)
        dma = pltpu.SemaphoreType.DMA

        def vmem(*shape):
            return pltpu.VMEM(shape, f32)

        hbm = pl.BlockSpec(memory_space=pltpu.HBM)
        either = pl.BlockSpec(memory_space=pl.ANY)
        cells = layers * rows * across
        heated, adj, new, goff = pl.pallas_call(
            lambda *refs: kernel(n_space, groups, *refs),
            out_shape=[jax.ShapeDtypeStruct(s, f32) for s in (whole, whole, whole, plane)],
            in_specs=[pl.BlockSpec(memory_space=pltpu.SMEM)] + [hbm] * 8,
            out_specs=[either] * 4,
            scratch_shapes=[vmem(*whole)] * 4
            + [vmem(*plane)] * 5
            + [vmem(*whole)] * 6
            + [
                vmem(chunks, *plane),
                vmem(groups, chunks, *plane),
                vmem(chunks, *plane),
                vmem(2, 4, layers, across),
                vmem(2, 3, layers, across),
                vmem(2, 2, layers, across),
                vmem(CORES, extra, across),
                vmem(extra, across),
                vmem(groups, extra, across),
                vmem(*plane),
                dma((8,)),
                dma((2,)),
                dma((2,)),
                dma((chunks + 1,)),
                dma((chunks + 1,)),
                dma((max(groups - 1, 1), chunks + 1)),
                dma((groups, chunks + 1)),
                dma((chunks + 1,)),
                dma((chunks + 1,)),
                dma((chunks + 1,)),
                dma((2, layers)),
            ],
            compiler_params=pltpu.CompilerParams(
                collective_id=0, has_side_effects=True, vmem_limit_bytes=62 * 1024 * 1024
            ),
            cost_estimate=pl.CostEstimate(
                flops=100 * cells, bytes_accessed=28 * cells, transcendentals=3 * cells
            ),
            name="heat_step",
        )(
            tile_len,
            start_temp[0],
            porosity,
            cotangent[0],
            conductivity,
            surface_temp[0],
            surface_offset,
            basal_flux,
            thickness,
        )
        return heated[None], adj[None], new, goff

    in_specs = (
        P("member", None, "space", None),
        P("member", None, "space", None),
        P(None, "space", None),
        P(None, "space", None),
        P("member", "space", None),
        P("space", None),
        P("space", None),
        P("space", None),
        P("space"),
    )
    out_specs = (
        P("member", None, "space", None),
        P("member", None, "space", None),
        P(None, "space", None),
        P("space", None),
    )
    return jax.shard_map(body, mesh=mesh, in_specs=in_specs, out_specs=out_specs, check_vma=False)
```

time: 112 us -> 21.5 us (0.19)
  waiting for transfers between devices: 32.7 us -> 0 us
  local copies, waits for them, and re-layouts: 22.3 us -> 4.59 us
  other arithmetic: 16.8 us -> 0 us
  Pallas kernels: 0 us -> 15.4 us
  between operations: 15.2 us -> 1.3 us
  starting transfers between devices: 12.6 us -> 0 us
  blocking collectives: 11.4 us -> 0 us
    psum x1 -> x0, waiting for transfers between devices: 32.6 us -> none  [body(): total_k, total_off = lax.psum((grad_k, grad_off), 'member')]
    pallas_call x0 -> x1, Pallas kernels: none -> 15.4 us  [body(): pl.pallas_call(lambda *refs: kernel(n_space, groups, *refs), out_shape=[j...]
    ppermute x4 -> x0, starting transfers between devices: 12.5 us -> none  [from_behind(): return lax.ppermute(block, axis, route)]
    psum x1 -> x0, blocking collectives: 11.4 us -> none  [body(): total_k, total_off = lax.psum((grad_k, grad_off), 'member')]
    unnamed x65 -> x10, local copies, waits for them, and re-layouts: 13.4 us -> 4.59 us
    slice x11 -> x0, local copies, waits for them, and re-layouts: 7.75 us -> none  [the longest x2 2.25 us: tendency(): east_k = jnp.concatenate([cond[..., 1:], cond[..., -1:]], axis=-1)]
    add x4 -> x0, other arithmetic: 6.07 us -> none  [the longest x1 5.86 us: body(): grad_t = grad_t + jnp.where(at_end, back_last[0][:, None], 0.0)]
    mul x4 -> x0, other arithmetic: 5.73 us -> none  [the longest x2 2.41 us: tendency(): 0.5 * (cond + east_k) * (east_t - temp)]
  transfers between devices with their start and end apart: 5 -> 0, of which waited for: 1 -> 0; matrix products, arithmetic and copies ran while one was open for 23% -> 0% of each run, Pallas kernels for 0% -> 0%
where the time goes in v1:
time: 21.5 us; the launch traced here: 21.3 us
  Pallas kernels  15.4 us (72%)
  local copies, waits for them, and re-layouts  4.59 us (21%)
  between operations  1.3 us (6%)
    pallas_call x1, Pallas kernels, body(): pl.pallas_call(lambda *refs: kernel(n_space, groups, *refs), out_shape=[j...  15.4 us
    unnamed x10, local copies, waits for them, and re-layouts  4.59 us

profile of v1, /device:TPU:0, one launch (start us, length us, event | category | flops | bytes accessed | tf_op | source)
XLA Modules:
  0.0 21.3 jit_solution(1729107957740007306)
XLA Ops:
  1.3 15.4 %heat_step.1 = (f32[16,64,128]{2,1,0:T(8,128)}, f32[16,64,128]{2,1,0:T(8,128)}, f32[16,64,128]{2,1,0:T(8,128)}, f32[64,128]{1,0:T(8,128)}) custom-call(s32[1]{0:T(128)S(6)} %copy.17.refs_0_, f32[16,64,128]{2,1,0:T(8,128)} %bitcast.5, f32[16,64,128]{2,1,0:T(8,128)} %refs_2_.1, f32[16,64,128]{2,1,0:T(8,128)} %bitcast.6, f32[16,64,128]{2,1,0:T(8,128)} %refs_4_.1, ...), custom_call_target="tpu_custom_call" | custom-call | flops 13107200 | bytes 3670016 | tf_op jit(solution)/shard_map/heat_step/pallas_call | solution.py:493
  16.7 0.0 copy-start.1
  16.7 1.9 %copy.18 = f32[1,16,64,128]{3,2,1,0:T(8,128)} copy(f32[1,16,64,128]{3,2,1,0:T(8,128)} %bitcast.8) | data formatting | bytes 1048576
  18.6 0.0 copy-done.1
  18.6 0.0 copy-start
  18.6 0.8 %copy.19 = f32[1,16,64,128]{3,2,1,0:T(8,128)} copy(f32[1,16,64,128]{3,2,1,0:T(8,128)S(1)} %bitcast.7) | data formatting | bytes 1048576
  19.4 0.4 %copy-done = f32[16,64,128]{2,1,0:T(8,128)S(1)} copy-done((f32[16,64,128]{2,1,0:T(8,128)S(1)}, f32[16,64,128]{2,1,0:T(8,128)}, u32[]{:S(2)}) %copy-start) | copy-done | bytes 524312
  19.8 0.0 copy-start.2
  19.8 0.8 %copy.20 = f32[16,64,128]{2,1,0:T(8,128)} copy(f32[16,64,128]{2,1,0:T(8,128)S(1)} %copy-done) | data formatting | bytes 1048576
  20.6 0.0 copy-done.2
  20.6 0.6 %copy.21 = f32[64,128]{1,0:T(8,128)} copy(f32[64,128]{1,0:T(8,128)S(1)} %copy-done.2) | data formatting | bytes 65536
Async XLA Ops:
  16.7 2.0 %copy-start.1 = (f32[16,64,128]{2,1,0:T(8,128)S(1)}, f32[16,64,128]{2,1,0:T(8,128)}, u32[]{:S(2)}) copy-start(f32[16,64,128]{2,1,0:T(8,128)} %get-tuple-element.9) | copy-start | bytes 1572868
  18.6 1.2 %copy-start = (f32[16,64,128]{2,1,0:T(8,128)S(1)}, f32[16,64,128]{2,1,0:T(8,128)}, u32[]{:S(2)}) copy-start(f32[16,64,128]{2,1,0:T(8,128)} %get-tuple-element.18) | copy-start | bytes 1572868
  19.8 0.8 %copy-start.2 = (f32[64,128]{1,0:T(8,128)S(1)}, f32[64,128]{1,0:T(8,128)}, u32[]{:S(2)}) copy-start(f32[64,128]{1,0:T(8,128)} %get-tuple-element.19) | copy-start | bytes 98308

commit v2 on v1

--- a/solution.py
+++ b/solution.py
@@ -23,10 +23,10 @@
     offset_hbm,
     basal_hbm,
     thick_hbm,
-    heated_hbm,
-    adj_hbm,
-    new_hbm,
-    goff_hbm,
+    heated,
+    adj,
+    new,
+    goff,
     temp,
     por,
     cot,
@@ -39,19 +39,16 @@
     weight,
     recip,
     slope,
-    heated,
-    adj,
     grad,
     near,
     far,
-    new,
     edge_out,
     edge_in,
     edge,
     extra_out,
     extra_near,
     extra_far,
-    goff,
+    goff_mine,
     in_sem,
     halo_send,
     halo_recv,
@@ -61,8 +58,6 @@
     far_recv,
     new_send,
     new_recv,
-    new_local,
-    out_sem,
 ):
     layers, rows, across = temp.shape
     chunks = layers // CORES
@@ -91,24 +86,29 @@
     def _():
         pl.semaphore_signal(barrier, inc=1, device_id=ahead, device_id_type=MESH)
 
+    early = 2 * CORES
+    fields = [(temp_hbm, temp), (por_hbm, por), (cot_hbm, cot), (cond_hbm, cond)]
+    planes = [(thick_hbm, thick), (surf_hbm, surf), (offset_hbm, offset), (basal_hbm, basal)]
+    pieces = [(src.at[0:early], dst.at[0:early]) for src, dst in fields]
+    pieces += planes
+    n_first = len(pieces)
+    pieces += [(src.at[early:layers], dst.at[early:layers]) for src, dst in fields]
     loads = [
-        pltpu.make_async_copy(src, dst, in_sem.at[i])
-        for i, (src, dst) in enumerate(
-            [
-                (temp_hbm, temp),
-                (por_hbm, por),
-                (cot_hbm, cot),
-                (cond_hbm, cond),
-                (surf_hbm, surf),
-                (offset_hbm, offset),
-                (basal_hbm, basal),
-                (thick_hbm, thick),
-            ]
-        )
+        pltpu.make_async_copy(src, dst, in_sem.at[i]) for i, (src, dst) in enumerate(pieces)
     ]
     for load in loads:
         load.start()
 
+    @pl.when(jnp.logical_not(has_behind))
+    def _():
+        edge_in[0] = jnp.zeros(edge_in.shape[1:], jnp.float32)
+
+    @pl.when(jnp.logical_not(has_ahead))
+    def _():
+        edge_in[1] = jnp.zeros(edge_in.shape[1:], jnp.float32)
+
+    for load in loads[:n_first]:
+        load.wait()
     count = len_ref[0]
     end = jnp.clip(count - 1, 0, rows - 1)
     row = lax.broadcasted_iota(jnp.int32, (rows, across), 0)
@@ -116,35 +116,13 @@
     live = row < count
     inner = (row >= 1) & live
     not_east = col < across - 1
-
-    @pl.when(jnp.logical_not(has_behind))
-    def _():
-        edge_in[0] = jnp.zeros(edge_in.shape[1:], jnp.float32)
-
-    @pl.when(jnp.logical_not(has_ahead))
-    def _():
-        edge_in[1] = jnp.zeros(edge_in.shape[1:], jnp.float32)
-
-    for load in loads:
-        load.wait()
+    inverse[...] = 1.0 / (thick[...] * thick[...])
 
     def pointwise(v, p, c):
         th = jnp.tanh(v)
         q = p * (1.0 - th * th)
         r = 1.0 / (1.0 + 4.0 * q)
         return r, STEP * c * r, 8.0 * th * q
-
-    for layer in range(layers):
-        at = pl.ds(layer, 1)
-        for f, field in enumerate((temp, cond, cot, por)):
-            edge_out[0, f, at, :] = field[layer, 0:1, :]
-            edge_out[1, f, at, :] = field[layer, pl.ds(end, 1), :]
-    for side in range(2):
-        _, w, _ = pointwise(edge_out[side, 0], edge_out[side, 3], edge_out[side, 2])
-        edge_out[side, 2] = w
-
-    neighbours = has_behind.astype(jnp.int32) + has_ahead.astype(jnp.int32)
-    pl.semaphore_wait(barrier, groups + neighbours)
 
     to_behind = pltpu.make_async_remote_copy(
         src_ref=edge_out.at[0, 0:3],
@@ -162,16 +140,6 @@
         device_id=ahead,
         device_id_type=MESH,
     )
-
-    @pl.when(has_behind)
-    def _():
-        to_behind.start()
-
-    @pl.when(has_ahead)
-    def _():
-        to_ahead.start()
-
-    inverse[...] = 1.0 / (thick[...] * thick[...])
 
     def weigh(layer):
         r, w, s = pointwise(temp[layer], por[layer], cot[layer])
@@ -228,7 +196,7 @@
             f = f + a * dv
             b = b - a * w
             g = g - 4.0 * (dv * w)
-            goff[...] = a * inv * w
+            goff_mine[...] = a * inv * w
         flow = flow + f * inv
         back = back + b * inv
         cross = cross + g * inv
@@ -237,6 +205,8 @@
         heated[layer] = flow
         adj[layer] = back
         grad[layer] = -0.5 * cross
+
+    neighbours = has_behind.astype(jnp.int32) + has_ahead.astype(jnp.int32)
 
     def near_copy(j):
         return pltpu.make_async_remote_copy(
@@ -281,6 +251,8 @@
             weigh(layer + 3)
         stencil(layer, None if first else layer - 1, layer + 1, top=first)
         stencil(layer + 1, layer, None if last else layer + 2, bottom=last)
+        if first:
+            pl.semaphore_wait(barrier, groups + neighbours)
         near_copy(j).start()
 
     def pass_on(j):
@@ -316,6 +288,26 @@
     weigh(0)
     weigh(1)
     chunk(0, first=True)
+    for load in loads[n_first:]:
+        load.wait()
+
+    for layer in range(layers):
+        at = pl.ds(layer, 1)
+        for f, field in enumerate((temp, cond, cot, por)):
+            edge_out[0, f, at, :] = field[layer, 0:1, :]
+            edge_out[1, f, at, :] = field[layer, pl.ds(end, 1), :]
+    for side in range(2):
+        _, w, _ = pointwise(edge_out[side, 0], edge_out[side, 3], edge_out[side, 2])
+        edge_out[side, 2] = w
+
+    @pl.when(has_behind)
+    def _():
+        to_behind.start()
+
+    @pl.when(has_ahead)
+    def _():
+        to_ahead.start()
+
     middle = chunks // 2
     lax.fori_loop(1, middle, step, 0)
 
@@ -338,7 +330,7 @@
             at = side * chunks + layer // CORES
             extra_out[layer % CORES, at : at + 1, :] = g[layer : layer + 1, :]
     for h in range(CORES):
-        extra_out[h, layers : layers + half, :] = goff[h * half : (h + 1) * half, :]
+        extra_out[h, layers : layers + half, :] = goff_mine[h * half : (h + 1) * half, :]
     extra_near_copy.start()
 
     lax.fori_loop(middle, chunks - 1, step, 0)
@@ -352,12 +344,6 @@
     first_row = row == 0
     last_row = row == count - 1
 
-    def out_copies(layer):
-        return (
-            pltpu.make_async_copy(heated.at[layer], heated_hbm.at[layer], out_sem.at[0, layer]),
-            pltpu.make_async_copy(adj.at[layer], adj_hbm.at[layer], out_sem.at[1, layer]),
-        )
-
     def finish(layer, carry):
         at = pl.ds(layer, 1)
 
@@ -371,8 +357,6 @@
         adj[layer] = jnp.where(
             live, cot[layer] + (adj[layer] + edges(1) + slope[layer] * flow), 0.0
         )
-        for copy in out_copies(layer):
-            copy.start()
         return carry
 
     lax.fori_loop(0, 4, finish, 0)
@@ -386,32 +370,38 @@
         total = total + extra_far[p]
     extra_near[...] = total
     mine = pl.ds(pl.multiple_of(core * half, half), half)
-    goff_local = pltpu.make_async_copy(
-        extra_near.at[pl.ds(layers, half)], goff_hbm.at[mine], new_local.at[chunks]
-    )
+    other = pl.ds(pl.multiple_of((1 - core) * half, half), half)
+    goff[mine, :] = total[layers : layers + half]
     goff_remote = pltpu.make_async_remote_copy(
-        src_ref=extra_near.at[pl.ds(layers, half)],
-        dst_ref=goff_hbm.at[mine],
+        src_ref=goff.at[mine],
+        dst_ref=goff.at[mine],
         send_sem=new_send.at[chunks],
         recv_sem=new_recv.at[chunks],
         device_id=partner,
         device_id_type=MESH,
     )
-    goff_local.start()
     goff_remote.start()
 
-    def new_copies(j):
+    def new_copy(j):
         layer = CORES * j + core
-        return (
-            pltpu.make_async_copy(new.at[j], new_hbm.at[layer], new_local.at[j]),
-            pltpu.make_async_remote_copy(
-                src_ref=new.at[j],
-                dst_ref=new_hbm.at[layer],
-                send_sem=new_send.at[j],
-                recv_sem=new_recv.at[j],
-                device_id=partner,
-                device_id_type=MESH,
-            ),
+        return pltpu.make_async_remote_copy(
+            src_ref=new.at[layer],
+            dst_ref=new.at[layer],
+            send_sem=new_send.at[j],
+            recv_sem=new_recv.at[j],
+            device_id=partner,
+            device_id_type=MESH,
+        )
+
+    def new_arrival(j):
+        layer = CORES * j + 1 - core
+        return pltpu.make_async_remote_copy(
+            src_ref=new.at[layer],
+            dst_ref=new.at[layer],
+            send_sem=new_send.at[j],
+            recv_sem=new_recv.at[j],
+            device_id=partner,
+            device_id_type=MESH,
         )
 
     def update(j, carry):
@@ -422,9 +412,9 @@
             total = total + far[p, j]
         total = total + jnp.where(first_row, extra_near[pl.ds(j, 1), :], 0.0)
         total = total + jnp.where(last_row, extra_near[pl.ds(chunks + j, 1), :], 0.0)
-        new[j] = cond[CORES * j + core] * jnp.exp(-RATE * jnp.tanh(total))
-        for copy in new_copies(j):
-            copy.start()
+        layer = CORES * j + core
+        new[layer] = cond[layer] * jnp.exp(-RATE * jnp.tanh(total))
+        new_copy(j).start()
         return carry
 
     lax.fori_loop(0, chunks, update, 0)
@@ -433,14 +423,8 @@
         near_copy(j).wait_send()
         for copy in far_copies(j):
             copy.wait_send()
-        local, remote = new_copies(j)
-        local.wait()
-        remote.wait()
-        return carry
-
-    def drain_out(layer, carry):
-        for copy in out_copies(layer):
-            copy.wait()
+        new_copy(j).wait_send()
+        new_arrival(j).wait_recv()
         return carry
 
     @pl.when(has_behind)
@@ -454,10 +438,28 @@
     extra_near_copy.wait_send()
     for d in range(groups - 1):
         extra_far_copy(d, group).wait_send()
-    lax.fori_loop(0, layers, drain_out, 0)
     lax.fori_loop(0, chunks, drain, 0)
-    goff_local.wait()
-    goff_remote.wait()
+    goff_remote.wait_send()
+    pltpu.make_async_remote_copy(
+        src_ref=goff.at[other],
+        dst_ref=goff.at[other],
+        send_sem=new_send.at[chunks],
+        recv_sem=new_recv.at[chunks],
+        device_id=partner,
+        device_id_type=MESH,
+    ).wait_recv()
+
+
+def write_out(*refs):
+    sources, targets, sem = refs[:4], refs[4:8], refs[8]
+    copies = [
+        pltpu.make_async_copy(src, dst, sem.at[i])
+        for i, (src, dst) in enumerate(zip(sources, targets))
+    ]
+    for copy in copies:
+        copy.start()
+    for copy in copies:
+        copy.wait()
 
 
 def solution(mesh):
@@ -492,16 +494,15 @@
         cells = layers * rows * across
         heated, adj, new, goff = pl.pallas_call(
             lambda *refs: kernel(n_space, groups, *refs),
-            out_shape=[jax.ShapeDtypeStruct(s, f32) for s in (whole, whole, whole, plane)],
+            out_shape=[pltpu.VMEM(s, f32) for s in (whole, whole, whole, plane)],
             in_specs=[pl.BlockSpec(memory_space=pltpu.SMEM)] + [hbm] * 8,
-            out_specs=[either] * 4,
+            out_specs=[pl.BlockSpec(memory_space=pltpu.VMEM)] * 4,
             scratch_shapes=[vmem(*whole)] * 4
             + [vmem(*plane)] * 5
-            + [vmem(*whole)] * 6
+            + [vmem(*whole)] * 4
             + [
                 vmem(chunks, *plane),
                 vmem(groups, chunks, *plane),
-                vmem(chunks, *plane),
                 vmem(2, 4, layers, across),
                 vmem(2, 3, layers, across),
                 vmem(2, 2, layers, across),
@@ -509,7 +510,7 @@
                 vmem(extra, across),
                 vmem(groups, extra, across),
                 vmem(*plane),
-                dma((8,)),
+                dma((12,)),
                 dma((2,)),
                 dma((2,)),
                 dma((chunks + 1,)),
@@ -518,11 +519,9 @@
                 dma((groups, chunks + 1)),
                 dma((chunks + 1,)),
                 dma((chunks + 1,)),
-                dma((chunks + 1,)),
-                dma((2, layers)),
             ],
             compiler_params=pltpu.CompilerParams(
-                collective_id=0, has_side_effects=True, vmem_limit_bytes=62 * 1024 * 1024
+                collective_id=0, has_side_effects=True, vmem_limit_bytes=48 * 1024 * 1024
             ),
             cost_estimate=pl.CostEstimate(
                 flops=100 * cells, bytes_accessed=28 * cells, transcendentals=3 * cells
@@ -530,15 +529,29 @@
             name="heat_step",
         )(
             tile_len,
-            start_temp[0],
-            porosity,
-            cotangent[0],
-            conductivity,
-            surface_temp[0],
-            surface_offset,
-            basal_flux,
-            thickness,
+            *[
+                pltpu.with_memory_space_constraint(x, pltpu.HBM)
+                for x in (
+                    start_temp[0],
+                    porosity,
+                    cotangent[0],
+                    conductivity,
+                    surface_temp[0],
+                    surface_offset,
+                    basal_flux,
+                    thickness,
+                )
+            ]
         )
+        heated, adj, new, goff = pl.pallas_call(
+            write_out,
+            out_shape=[pltpu.HBM(s, f32) for s in (whole, whole, whole, plane)],
+            in_specs=[either] * 4,
+            out_specs=[hbm] * 4,
+            scratch_shapes=[dma((4,))],
+            cost_estimate=pl.CostEstimate(flops=0, bytes_accessed=24 * cells, transcendentals=0),
+            name="write_out",
+        )(heated, adj, new, goff)
         return heated[None], adj[None], new, goff
 
     in_specs = (

time: 21.5 us -> 69.3 us (3.22)
  Pallas kernels: 15.4 us -> 64.8 us
  local copies, waits for them, and re-layouts: 4.59 us -> 2.98 us
    pallas_call x1 -> x2, Pallas kernels: 15.4 us -> 64.8 us  [the longest x1 49.8 us: body(): pl.pallas_call(write_out, out_shape=[pltpu.HBM(s, f32) for s in (whole, w...]
    unnamed x10 -> x8, local copies, waits for them, and re-layouts: 4.59 us -> 2.98 us
where the time goes in v2:
time: 69.3 us; the launch traced here: 69.1 us
  Pallas kernels  64.8 us (94%)
  local copies, waits for them, and re-layouts  2.98 us (4%)
  between operations  1.3 us (2%)
    pallas_call x1, Pallas kernels, body(): pl.pallas_call(write_out, out_shape=[pltpu.HBM(s, f32) for s in (whole, w...  49.8 us
    pallas_call x1, Pallas kernels, body(): pl.pallas_call(lambda *refs: kernel(n_space, groups, *refs), out_shape=[p...  15.1 us
    unnamed x8, local copies, waits for them, and re-layouts  2.98 us

profile of v2, /device:TPU:0, one launch (start us, length us, event | category | flops | bytes accessed | tf_op | source)
XLA Modules:
  0.0 69.1 jit_solution(18346785545658614517)
XLA Ops:
  1.3 15.1 %heat_step.1 = (f32[16,64,128]{2,1,0:T(8,128)S(1)}, f32[16,64,128]{2,1,0:T(8,128)S(1)}, f32[16,64,128]{2,1,0:T(8,128)S(1)}, f32[64,128]{1,0:T(8,128)S(1)}) custom-call(s32[1]{0:T(128)S(6)} %copy.13.refs_0_, f32[16,64,128]{2,1,0:T(8,128)} %bitcast.5, f32[16,64,128]{2,1,0:T(8,128)} %refs_2_.1, f32[16,64,128]{2,1,0:T(8,128)} %bitcast.6, ...), custom_call_target="tpu_custom_call" | custom-call | flops 13107200 | bytes 3670016 | tf_op jit(solution)/shard_map/heat_step/pallas_call | solution.py:495
  16.3 0.0 copy-start
  16.4 0.8 %copy-done = f32[16,64,128]{2,1,0:T(8,128)} copy-done((f32[16,64,128]{2,1,0:T(8,128)}, f32[16,64,128]{2,1,0:T(8,128)S(1)}, u32[]{:S(2)}) %copy-start) | copy-done | bytes 524312
  17.1 0.0 copy-start.1
  17.1 0.8 %copy-done.1 = f32[16,64,128]{2,1,0:T(8,128)} copy-done((f32[16,64,128]{2,1,0:T(8,128)}, f32[16,64,128]{2,1,0:T(8,128)S(1)}, u32[]{:S(2)}) %copy-start.1) | copy-done | bytes 524312
  17.9 0.0 copy-start.2
  17.9 0.8 %copy-done.2 = f32[16,64,128]{2,1,0:T(8,128)} copy-done((f32[16,64,128]{2,1,0:T(8,128)}, f32[16,64,128]{2,1,0:T(8,128)S(1)}, u32[]{:S(2)}) %copy-start.2) | copy-done | bytes 524312
  18.7 0.0 copy-start.3
  18.7 0.6 copy-done.3
  19.3 49.8 %write_out.1 = (f32[16,64,128]{2,1,0:T(8,128)}, f32[16,64,128]{2,1,0:T(8,128)}, f32[16,64,128]{2,1,0:T(8,128)}, f32[64,128]{1,0:T(8,128)}) custom-call(f32[16,64,128]{2,1,0:T(8,128)} %copy-done, f32[16,64,128]{2,1,0:T(8,128)} %copy-done.1, f32[16,64,128]{2,1,0:T(8,128)} %copy-done.2, f32[64,128]{1,0:T(8,128)} %copy-done.3), custom_call_target="tpu_custom_call" | custom-call | bytes 3145728 | tf_op jit(solution)/shard_map/write_out/pallas_call | solution.py:546
Async XLA Ops:
  16.3 0.8 %copy-start = (f32[16,64,128]{2,1,0:T(8,128)}, f32[16,64,128]{2,1,0:T(8,128)S(1)}, u32[]{:S(2)}) copy-start(f32[16,64,128]{2,1,0:T(8,128)S(1)} %get-tuple-element.12.refs_0_) | copy-start | bytes 1572868
  17.1 0.8 %copy-start.1 = (f32[16,64,128]{2,1,0:T(8,128)}, f32[16,64,128]{2,1,0:T(8,128)S(1)}, u32[]{:S(2)}) copy-start(f32[16,64,128]{2,1,0:T(8,128)S(1)} %get-tuple-element.13.refs_1_) | copy-start | bytes 1572868
  17.9 0.8 %copy-start.2 = (f32[16,64,128]{2,1,0:T(8,128)}, f32[16,64,128]{2,1,0:T(8,128)S(1)}, u32[]{:S(2)}) copy-start(f32[16,64,128]{2,1,0:T(8,128)S(1)} %get-tuple-element.14.refs_2_) | copy-start | bytes 1572868
  18.7 0.6 copy-start.3

commit v3 on v2

--- a/solution.py
+++ b/solution.py
@@ -86,18 +86,20 @@
     def _():
         pl.semaphore_signal(barrier, inc=1, device_id=ahead, device_id_type=MESH)
 
-    early = 2 * CORES
+    cuts = [0, 2 * CORES, 4 * CORES, layers]
     fields = [(temp_hbm, temp), (por_hbm, por), (cot_hbm, cot), (cond_hbm, cond)]
     planes = [(thick_hbm, thick), (surf_hbm, surf), (offset_hbm, offset), (basal_hbm, basal)]
-    pieces = [(src.at[0:early], dst.at[0:early]) for src, dst in fields]
-    pieces += planes
-    n_first = len(pieces)
-    pieces += [(src.at[early:layers], dst.at[early:layers]) for src, dst in fields]
+    parts = [
+        [(src.at[lo:hi], dst.at[lo:hi]) for src, dst in fields] for lo, hi in zip(cuts, cuts[1:])
+    ]
+    parts[0] += planes
     loads = [
-        pltpu.make_async_copy(src, dst, in_sem.at[i]) for i, (src, dst) in enumerate(pieces)
+        [pltpu.make_async_copy(src, dst, in_sem.at[p, i]) for i, (src, dst) in enumerate(part)]
+        for p, part in enumerate(parts)
     ]
-    for load in loads:
-        load.start()
+    for part in loads:
+        for load in part:
+            load.start()
 
     @pl.when(jnp.logical_not(has_behind))
     def _():
@@ -107,7 +109,7 @@
     def _():
         edge_in[1] = jnp.zeros(edge_in.shape[1:], jnp.float32)
 
-    for load in loads[:n_first]:
+    for load in loads[0]:
         load.wait()
     count = len_ref[0]
     end = jnp.clip(count - 1, 0, rows - 1)
@@ -263,7 +265,7 @@
 
     def step(j, carry):
         chunk(j)
-        pass_on(j - 1)
+        pass_on(j - 2)
         return carry
 
     extra_near_copy = pltpu.make_async_remote_copy(
@@ -288,7 +290,10 @@
     weigh(0)
     weigh(1)
     chunk(0, first=True)
-    for load in loads[n_first:]:
+    for load in loads[1]:
+        load.wait()
+    chunk(1)
+    for load in loads[2]:
         load.wait()
 
     for layer in range(layers):
@@ -309,7 +314,7 @@
         to_ahead.start()
 
     middle = chunks // 2
-    lax.fori_loop(1, middle, step, 0)
+    lax.fori_loop(2, middle, step, 0)
 
     @pl.when(has_ahead)
     def _():
@@ -339,7 +344,7 @@
     for d in range(groups - 1):
         extra_far_copy(d, group).start()
     chunk(chunks - 1, last=True)
-    pass_on(chunks - 2)
+    pass_on(chunks - 3)
 
     first_row = row == 0
     last_row = row == count - 1
@@ -359,6 +364,7 @@
         )
         return carry
 
+    pass_on(chunks - 2)
     lax.fori_loop(0, 4, finish, 0)
     pass_on(chunks - 1)
     lax.fori_loop(4, layers, finish, 0)
@@ -490,7 +496,6 @@
             return pltpu.VMEM(shape, f32)
 
         hbm = pl.BlockSpec(memory_space=pltpu.HBM)
-        either = pl.BlockSpec(memory_space=pl.ANY)
         cells = layers * rows * across
         heated, adj, new, goff = pl.pallas_call(
             lambda *refs: kernel(n_space, groups, *refs),
@@ -510,7 +515,7 @@
                 vmem(extra, across),
                 vmem(groups, extra, across),
                 vmem(*plane),
-                dma((12,)),
+                dma((3, 8)),
                 dma((2,)),
                 dma((2,)),
                 dma((chunks + 1,)),
@@ -546,12 +551,12 @@
         heated, adj, new, goff = pl.pallas_call(
             write_out,
             out_shape=[pltpu.HBM(s, f32) for s in (whole, whole, whole, plane)],
-            in_specs=[either] * 4,
+            in_specs=[pl.BlockSpec(memory_space=pltpu.VMEM)] * 4,
             out_specs=[hbm] * 4,
             scratch_shapes=[dma((4,))],
             cost_estimate=pl.CostEstimate(flops=0, bytes_accessed=24 * cells, transcendentals=0),
             name="write_out",
-        )(heated, adj, new, goff)
+        )(*[pltpu.with_memory_space_constraint(x, pltpu.VMEM) for x in (heated, adj, new, goff)])
         return heated[None], adj[None], new, goff
 
     in_specs = (

time: 69.3 us -> 18.3 us (0.26)
  Pallas kernels: 64.8 us -> 16.9 us
  local copies, waits for them, and re-layouts: 2.98 us -> 0 us
    pallas_call x1, Pallas kernels: 49.8 us -> 1.18 us  [body(): pl.pallas_call(write_out, out_shape=[pltpu.HBM(s, f32) for s in (whole, w...]
    unnamed x8 -> x0, local copies, waits for them, and re-layouts: 2.98 us -> none
where the time goes in v3:
time: 18.3 us; the launch traced here: 18.2 us
  Pallas kernels  16.9 us (92%)
  between operations  1.29 us (7%)
    pallas_call x1, Pallas kernels, body(): pl.pallas_call(lambda *refs: kernel(n_space, groups, *refs), out_shape=[p...  15.7 us
    pallas_call x1, Pallas kernels, body(): pl.pallas_call(write_out, out_shape=[pltpu.HBM(s, f32) for s in (whole, w...  1.18 us

profile of v3, /device:TPU:0, one launch (start us, length us, event | category | flops | bytes accessed | tf_op | source)
XLA Modules:
  0.0 18.2 jit_solution(10713126879793495917)
XLA Ops:
  1.3 15.7 %heat_step.1 = (f32[16,64,128]{2,1,0:T(8,128)S(1)}, f32[16,64,128]{2,1,0:T(8,128)S(1)}, f32[16,64,128]{2,1,0:T(8,128)S(1)}, f32[64,128]{1,0:T(8,128)S(1)}) custom-call(s32[1]{0:T(128)S(6)} %copy.13.refs_0_, f32[16,64,128]{2,1,0:T(8,128)} %bitcast.5, f32[16,64,128]{2,1,0:T(8,128)} %refs_2_.1, f32[16,64,128]{2,1,0:T(8,128)} %bitcast.6, ...), custom_call_target="tpu_custom_call" | custom-call | flops 13107200 | bytes 3670016 | tf_op jit(solution)/shard_map/heat_step/pallas_call | solution.py:500
  17.0 1.2 %write_out.1 = (f32[16,64,128]{2,1,0:T(8,128)}, f32[16,64,128]{2,1,0:T(8,128)}, f32[16,64,128]{2,1,0:T(8,128)}, f32[64,128]{1,0:T(8,128)}) custom-call(f32[16,64,128]{2,1,0:T(8,128)S(1)} %get-tuple-element.12.refs_0_, f32[16,64,128]{2,1,0:T(8,128)S(1)} %get-tuple-element.13.refs_1_, f32[16,64,128]{2,1,0:T(8,128)S(1)} %get-tuple-element.14.refs_2_, ...), custom_call_target="tpu_custom_call" | custom-call | bytes 3145728 | tf_op jit(solution)/shard_map/write_out/pallas_call | solution.py:551

commit v4 on v3

--- a/solution.py
+++ b/solution.py
@@ -150,7 +150,7 @@
         weight[layer] = w
         slope[layer] = w * r * s
 
-    def stencil(layer, above, below, top=False, bottom=False):
+    def lateral(layer):
         v, k, w = temp[layer], cond[layer], weight[layer]
 
         def east(x):
@@ -165,7 +165,7 @@
         def following(x):
             return pltpu.roll(x, rows - 1, 0)
 
-        a = jnp.where(not_east, 0.5 * (k + east(k)), 0.0)
+        a = jnp.where(not_east, k + east(k), 0.0)
         dv = jnp.where(not_east, east(v) - v, 0.0)
         dw = east(w) - w
         f, b, g = a * dv, a * dw, dv * dw
@@ -173,40 +173,28 @@
         back = b - west(b)
         cross = g + west(g)
 
-        a = jnp.where(inner, 0.5 * (k + prev(k)), 0.0)
+        a = jnp.where(inner, k + prev(k), 0.0)
         dv = jnp.where(inner, prev(v) - v, 0.0)
         dw = prev(w) - w
         f, b, g = a * dv, a * dw, dv * dw
         flow = flow + (f - following(f))
         back = back + (b - following(b))
         cross = cross + (g + following(g))
-
-        parts = []
-        for other in (above, below):
-            if other is not None:
-                a = 0.5 * (k + cond[other])
-                dv = temp[other] - v
-                dw = weight[other] - w
-                parts.append((a * dv, a * dw, dv * dw))
-        f, b, g = parts[0]
-        for more in parts[1:]:
-            f, b, g = f + more[0], b + more[1], g + more[2]
+        return flow, back, cross
+
+    def face(layer):
+        a = cond[layer] + cond[layer + 1]
+        dv = temp[layer + 1] - temp[layer]
+        dw = weight[layer + 1] - weight[layer]
+        return a * dv, a * dw, dv * dw
+
+    def store(layer, side, vertical):
+        flow, back, cross = side
+        f, b, g = vertical
         inv = inverse[...]
-        if top:
-            a = 2.0 * k
-            dv = surf[...] + offset[...] - v
-            f = f + a * dv
-            b = b - a * w
-            g = g - 4.0 * (dv * w)
-            goff_mine[...] = a * inv * w
-        flow = flow + f * inv
-        back = back + b * inv
-        cross = cross + g * inv
-        if bottom:
-            flow = flow + basal[...] / thick[...]
-        heated[layer] = flow
-        adj[layer] = back
-        grad[layer] = -0.5 * cross
+        heated[layer] = 0.5 * (flow + f * inv)
+        adj[layer] = 0.5 * (back + b * inv)
+        grad[layer] = -0.5 * (cross + g * inv)
 
     neighbours = has_behind.astype(jnp.int32) + has_ahead.astype(jnp.int32)
 
@@ -250,12 +238,32 @@
         layer = CORES * j
         if not last:
             weigh(layer + 2)
-            weigh(layer + 3)
-        stencil(layer, None if first else layer - 1, layer + 1, top=first)
-        stencil(layer + 1, layer, None if last else layer + 2, bottom=last)
+        middle_face = face(layer)
+        f, b, g = middle_face
+        if first:
+            v, k, w = temp[layer], cond[layer], weight[layer]
+            dv = surf[...] + offset[...] - v
+            f = f + 4.0 * (k * dv)
+            b = b - 4.0 * (k * w)
+            g = g - 4.0 * (dv * w)
+            goff_mine[...] = 2.0 * (k * inverse[...] * w)
+        else:
+            upper = face(layer - 1)
+            f, b, g = f - upper[0], b - upper[1], g + upper[2]
+        store(layer, lateral(layer), (f, b, g))
+        f, b, g = middle_face
+        f, b = -f, -b
+        if not last:
+            lower = face(layer + 1)
+            f, b, g = f + lower[0], b + lower[1], g + lower[2]
+        store(layer + 1, lateral(layer + 1), (f, b, g))
+        if last:
+            heated[layer + 1] += basal[...] / thick[...]
         if first:
             pl.semaphore_wait(barrier, groups + neighbours)
         near_copy(j).start()
+        if not last:
+            weigh(layer + 3)
 
     def pass_on(j):
         near_copy(j).wait_recv()
@@ -265,7 +273,11 @@
 
     def step(j, carry):
         chunk(j)
-        pass_on(j - 2)
+
+        @pl.when(j > 2)
+        def _():
+            pass_on(j - 1)
+
         return carry
 
     extra_near_copy = pltpu.make_async_remote_copy(
@@ -293,6 +305,7 @@
     for load in loads[1]:
         load.wait()
     chunk(1)
+    pass_on(0)
     for load in loads[2]:
         load.wait()
 
@@ -313,6 +326,7 @@
     def _():
         to_ahead.start()
 
+    pass_on(1)
     middle = chunks // 2
     lax.fori_loop(2, middle, step, 0)
 
@@ -344,7 +358,6 @@
     for d in range(groups - 1):
         extra_far_copy(d, group).start()
     chunk(chunks - 1, last=True)
-    pass_on(chunks - 3)
 
     first_row = row == 0
     last_row = row == count - 1

time: 18.3 us -> 18.3 us (level)
  no operation moved by 1% of the time
where the time goes in v4:
time: 18.3 us; the launch traced here: 18.2 us
  Pallas kernels  16.9 us (92%)
  between operations  1.29 us (7%)
    pallas_call x1, Pallas kernels, body(): pl.pallas_call(lambda *refs: kernel(n_space, groups, *refs), out_shape=[p...  15.7 us
    pallas_call x1, Pallas kernels, body(): pl.pallas_call(write_out, out_shape=[pltpu.HBM(s, f32) for s in (whole, w...  1.18 us

profile of v4, /device:TPU:0, one launch (start us, length us, event | category | flops | bytes accessed | tf_op | source)
XLA Modules:
  0.0 18.2 jit_solution(9821472142859206852)
XLA Ops:
  1.3 15.7 %heat_step.1 = (f32[16,64,128]{2,1,0:T(8,128)S(1)}, f32[16,64,128]{2,1,0:T(8,128)S(1)}, f32[16,64,128]{2,1,0:T(8,128)S(1)}, f32[64,128]{1,0:T(8,128)S(1)}) custom-call(s32[1]{0:T(128)S(6)} %copy.13.refs_0_, f32[16,64,128]{2,1,0:T(8,128)} %bitcast.5, f32[16,64,128]{2,1,0:T(8,128)} %refs_2_.1, f32[16,64,128]{2,1,0:T(8,128)} %bitcast.6, ...), custom_call_target="tpu_custom_call" | custom-call | flops 13107200 | bytes 3670016 | tf_op jit(solution)/shard_map/heat_step/pallas_call | solution.py:513
  17.0 1.2 %write_out.1 = (f32[16,64,128]{2,1,0:T(8,128)}, f32[16,64,128]{2,1,0:T(8,128)}, f32[16,64,128]{2,1,0:T(8,128)}, f32[64,128]{1,0:T(8,128)}) custom-call(f32[16,64,128]{2,1,0:T(8,128)S(1)} %get-tuple-element.12.refs_0_, f32[16,64,128]{2,1,0:T(8,128)S(1)} %get-tuple-element.13.refs_1_, f32[16,64,128]{2,1,0:T(8,128)S(1)} %get-tuple-element.14.refs_2_, ...), custom_call_target="tpu_custom_call" | custom-call | bytes 3145728 | tf_op jit(solution)/shard_map/write_out/pallas_call | solution.py:564

commit v5 on v4

--- a/solution.py
+++ b/solution.py
@@ -251,6 +251,14 @@
             upper = face(layer - 1)
             f, b, g = f - upper[0], b - upper[1], g + upper[2]
         store(layer, lateral(layer), (f, b, g))
+        if not isinstance(j, int):
+
+            @pl.when(j > 3)
+            def _():
+                pass_on(j - 2)
+
+        elif j > 3:
+            pass_on(j - 2)
         f, b, g = middle_face
         f, b = -f, -b
         if not last:
@@ -273,11 +281,6 @@
 
     def step(j, carry):
         chunk(j)
-
-        @pl.when(j > 2)
-        def _():
-            pass_on(j - 1)
-
         return carry
 
     extra_near_copy = pltpu.make_async_remote_copy(
@@ -327,8 +330,9 @@
         to_ahead.start()
 
     pass_on(1)
-    middle = chunks // 2
-    lax.fori_loop(2, middle, step, 0)
+    lax.fori_loop(2, chunks - 1, step, 0)
+    chunk(chunks - 1, last=True)
+    pass_on(chunks - 2)
 
     @pl.when(has_ahead)
     def _():
@@ -352,13 +356,6 @@
         extra_out[h, layers : layers + half, :] = goff_mine[h * half : (h + 1) * half, :]
     extra_near_copy.start()
 
-    lax.fori_loop(middle, chunks - 1, step, 0)
-    extra_near_copy.wait_recv()
-    extra_far[group] = extra_out[core] + extra_near[...]
-    for d in range(groups - 1):
-        extra_far_copy(d, group).start()
-    chunk(chunks - 1, last=True)
-
     first_row = row == 0
     last_row = row == count - 1
 
@@ -377,10 +374,29 @@
         )
         return carry
 
-    pass_on(chunks - 2)
-    lax.fori_loop(0, 4, finish, 0)
+    lax.fori_loop(0, 2, finish, 0)
     pass_on(chunks - 1)
-    lax.fori_loop(4, layers, finish, 0)
+    lax.fori_loop(2, 8, finish, 0)
+    extra_near_copy.wait_recv()
+    extra_far[group] = extra_out[core] + extra_near[...]
+    for d in range(groups - 1):
+        extra_far_copy(d, group).start()
+    lax.fori_loop(8, layers, finish, 0)
+
+    def sent(j, carry):
+        near_copy(j).wait_send()
+        return carry
+
+    lax.fori_loop(0, chunks, sent, 0)
+    extra_near_copy.wait_send()
+
+    @pl.when(has_behind)
+    def _():
+        to_behind.wait_send()
+
+    @pl.when(has_ahead)
+    def _():
+        to_ahead.wait_send()
 
     for d in range(groups - 1):
         extra_far_copy(d, peers[d]).wait_recv()
@@ -434,27 +450,17 @@
         layer = CORES * j + core
         new[layer] = cond[layer] * jnp.exp(-RATE * jnp.tanh(total))
         new_copy(j).start()
-        return carry
-
-    lax.fori_loop(0, chunks, update, 0)
-
-    def drain(j, carry):
-        near_copy(j).wait_send()
         for copy in far_copies(j):
             copy.wait_send()
+        return carry
+
+    lax.fori_loop(0, chunks, update, 0)
+
+    def drain(j, carry):
         new_copy(j).wait_send()
         new_arrival(j).wait_recv()
         return carry
 
-    @pl.when(has_behind)
-    def _():
-        to_behind.wait_send()
-
-    @pl.when(has_ahead)
-    def _():
-        to_ahead.wait_send()
-
-    extra_near_copy.wait_send()
     for d in range(groups - 1):
         extra_far_copy(d, group).wait_send()
     lax.fori_loop(0, chunks, drain, 0)

time: 18.3 us -> 17.3 us (0.945)
  Pallas kernels: 16.9 us -> 15.8 us
    pallas_call x1, Pallas kernels: 15.7 us -> 14.6 us  [body(): pl.pallas_call(lambda *refs: kernel(n_space, groups, *refs), out_shape=[p...]
where the time goes in v5:
time: 17.3 us; the launch traced here: 17.1 us
  Pallas kernels  15.8 us (91%)
  between operations  1.29 us (7%)
    pallas_call x1, Pallas kernels, body(): pl.pallas_call(lambda *refs: kernel(n_space, groups, *refs), out_shape=[p...  14.6 us
    pallas_call x1, Pallas kernels, body(): pl.pallas_call(write_out, out_shape=[pltpu.HBM(s, f32) for s in (whole, w...  1.18 us

profile of v5, /device:TPU:0, one launch (start us, length us, event | category | flops | bytes accessed | tf_op | source)
XLA Modules:
  0.0 17.1 jit_solution(10505168903125414118)
XLA Ops:
  1.3 14.6 %heat_step.1 = (f32[16,64,128]{2,1,0:T(8,128)S(1)}, f32[16,64,128]{2,1,0:T(8,128)S(1)}, f32[16,64,128]{2,1,0:T(8,128)S(1)}, f32[64,128]{1,0:T(8,128)S(1)}) custom-call(s32[1]{0:T(128)S(6)} %copy.13.refs_0_, f32[16,64,128]{2,1,0:T(8,128)} %bitcast.5, f32[16,64,128]{2,1,0:T(8,128)} %refs_2_.1, f32[16,64,128]{2,1,0:T(8,128)} %bitcast.6, ...), custom_call_target="tpu_custom_call" | custom-call | flops 13107200 | bytes 3670016 | tf_op jit(solution)/shard_map/heat_step/pallas_call | solution.py:519
  15.9 1.2 %write_out.1 = (f32[16,64,128]{2,1,0:T(8,128)}, f32[16,64,128]{2,1,0:T(8,128)}, f32[16,64,128]{2,1,0:T(8,128)}, f32[64,128]{1,0:T(8,128)}) custom-call(f32[16,64,128]{2,1,0:T(8,128)S(1)} %get-tuple-element.12.refs_0_, f32[16,64,128]{2,1,0:T(8,128)S(1)} %get-tuple-element.13.refs_1_, f32[16,64,128]{2,1,0:T(8,128)S(1)} %get-tuple-element.14.refs_2_, ...), custom_call_target="tpu_custom_call" | custom-call | bytes 3145728 | tf_op jit(solution)/shard_map/write_out/pallas_call | solution.py:570

commit v6 on v5

--- a/solution.py
+++ b/solution.py
@@ -281,6 +281,11 @@
 
     def step(j, carry):
         chunk(j)
+
+        @pl.when(j == 2)
+        def _():
+            pass_on(1)
+
         return carry
 
     extra_near_copy = pltpu.make_async_remote_copy(
@@ -305,11 +310,7 @@
     weigh(0)
     weigh(1)
     chunk(0, first=True)
-    for load in loads[1]:
-        load.wait()
-    chunk(1)
-    pass_on(0)
-    for load in loads[2]:
+    for load in loads[1] + loads[2]:
         load.wait()
 
     for layer in range(layers):
@@ -329,10 +330,8 @@
     def _():
         to_ahead.start()
 
-    pass_on(1)
-    lax.fori_loop(2, chunks - 1, step, 0)
-    chunk(chunks - 1, last=True)
-    pass_on(chunks - 2)
+    pass_on(0)
+    lax.fori_loop(1, chunks - 1, step, 0)
 
     @pl.when(has_ahead)
     def _():
@@ -355,6 +354,12 @@
     for h in range(CORES):
         extra_out[h, layers : layers + half, :] = goff_mine[h * half : (h + 1) * half, :]
     extra_near_copy.start()
+    chunk(chunks - 1, last=True)
+    pass_on(chunks - 2)
+    extra_near_copy.wait_recv()
+    extra_far[group] = extra_out[core] + extra_near[...]
+    for d in range(groups - 1):
+        extra_far_copy(d, group).start()
 
     first_row = row == 0
     last_row = row == count - 1
@@ -376,12 +381,7 @@
 
     lax.fori_loop(0, 2, finish, 0)
     pass_on(chunks - 1)
-    lax.fori_loop(2, 8, finish, 0)
-    extra_near_copy.wait_recv()
-    extra_far[group] = extra_out[core] + extra_near[...]
-    for d in range(groups - 1):
-        extra_far_copy(d, group).start()
-    lax.fori_loop(8, layers, finish, 0)
+    lax.fori_loop(2, layers, finish, 0)
 
     def sent(j, carry):
         near_copy(j).wait_send()

time: 17.3 us -> 17.6 us (1.017)
  Pallas kernels: 15.8 us -> 16.1 us
    pallas_call x1, Pallas kernels: 14.6 us -> 14.9 us  [body(): pl.pallas_call(lambda *refs: kernel(n_space, groups, *refs), out_shape=[p...]
where the time goes in v6:
time: 17.6 us; the launch traced here: 17.4 us
  Pallas kernels  16.1 us (91%)
  between operations  1.29 us (7%)
    pallas_call x1, Pallas kernels, body(): pl.pallas_call(lambda *refs: kernel(n_space, groups, *refs), out_shape=[p...  14.9 us
    pallas_call x1, Pallas kernels, body(): pl.pallas_call(write_out, out_shape=[pltpu.HBM(s, f32) for s in (whole, w...  1.18 us

profile of v6, /device:TPU:0, one launch (start us, length us, event | category | flops | bytes accessed | tf_op | source)
XLA Modules:
  0.0 17.4 jit_solution(2518898543860730652)
XLA Ops:
  1.3 14.9 %heat_step.1 = (f32[16,64,128]{2,1,0:T(8,128)S(1)}, f32[16,64,128]{2,1,0:T(8,128)S(1)}, f32[16,64,128]{2,1,0:T(8,128)S(1)}, f32[64,128]{1,0:T(8,128)S(1)}) custom-call(s32[1]{0:T(128)S(6)} %copy.13.refs_0_, f32[16,64,128]{2,1,0:T(8,128)} %bitcast.5, f32[16,64,128]{2,1,0:T(8,128)} %refs_2_.1, f32[16,64,128]{2,1,0:T(8,128)} %bitcast.6, ...), custom_call_target="tpu_custom_call" | custom-call | flops 13107200 | bytes 3670016 | tf_op jit(solution)/shard_map/heat_step/pallas_call | solution.py:519
  16.2 1.2 %write_out.1 = (f32[16,64,128]{2,1,0:T(8,128)}, f32[16,64,128]{2,1,0:T(8,128)}, f32[16,64,128]{2,1,0:T(8,128)}, f32[64,128]{1,0:T(8,128)}) custom-call(f32[16,64,128]{2,1,0:T(8,128)S(1)} %get-tuple-element.12.refs_0_, f32[16,64,128]{2,1,0:T(8,128)S(1)} %get-tuple-element.13.refs_1_, f32[16,64,128]{2,1,0:T(8,128)S(1)} %get-tuple-element.14.refs_2_, ...), custom_call_target="tpu_custom_call" | custom-call | bytes 3145728 | tf_op jit(solution)/shard_map/write_out/pallas_call | solution.py:570
